TPU v7x, 512 devices: a whole 4x4x16 slice. The times are simulated.
512 devices in a mesh: row: 16 (over z), col: 32 (over y, x, core).
Axes of the slice: x: 4, y: 4, z: 16, core: 2. Of those that a mesh axis runs over, the one named last changes fastest.
Arguments:
- inputs: bfloat16 [768, 12288], P('col', 'row'), may hold values from -40 to 40
- ln_gain: float32 [12288], P('row'), may hold values from 0.25 to 1.75
- ln_bias: float32 [12288], P('row'), may hold values from -4 to 4
- w_up: bfloat16 [12288, 49152], P('row', 'col'), may hold values from -0.0546875 to 0.0546875
- up_bias: float32 [49152], P('col'), may hold values from -4 to 4
- w_down: bfloat16 [49152, 12288], P('col', 'row'), may hold values from -0.02734375 to 0.02734375
- down_bias: float32 [12288], P('row'), may hold values from -4 to 4
Outputs:
- block_out: bfloat16 [768, 12288], P('col', 'row')
All inputs are finite; a program needn't handle non-finite values.
Results may differ from a plain program's by a relative error of at most 0.0085.
Values may be sent and summed in bfloat16 or wider, within the bound.
A program may use at most 64 MiB of HBM per device.

v0:
```python
import jax
import jax.numpy as jnp
from jax import lax
from jax.sharding import PartitionSpec as P

D = 12288


def local(inputs, ln_gain, ln_bias, w_up, up_bias, w_down, down_bias):
    in_float = inputs.astype(jnp.float32)
    total = lax.psum(jnp.sum(in_float, axis=1), "row")
    average = total / D
    centered = in_float - average[:, None]
    spread = lax.psum(jnp.sum(centered * centered, axis=1), "row")
    variance = spread / D
    normed = (centered * lax.rsqrt(variance + 1e-05)[:, None] * ln_gain + ln_bias).astype(
        jnp.bfloat16
    )
    gathered = lax.all_gather(normed, "col", axis=0, tiled=True)
    summed = lax.psum_scatter(
        jnp.dot(gathered, w_up, preferred_element_type=jnp.float32).astype(jnp.bfloat16),
        "row",
        scatter_dimension=0,
        tiled=True,
    ).astype(jnp.float32)
    hidden = jax.nn.gelu(summed + up_bias, approximate=True).astype(jnp.bfloat16)
    terms = jnp.dot(
        lax.all_gather(hidden, "row", axis=0, tiled=True),
        w_down,
        preferred_element_type=jnp.float32,
    )
    down_sum = lax.psum_scatter(
        terms.astype(jnp.bfloat16), "col", scatter_dimension=0, tiled=True
    ).astype(jnp.float32)
    return (in_float + down_sum + down_bias).astype(jnp.bfloat16)


def solution(mesh):
    placed = (
        P("col", "row"),
        P("row"),
        P("row"),
        P("row", "col"),
        P("col"),
        P("col", "row"),
        P("row"),
    )
    return jax.shard_map(
        local, mesh=mesh, in_specs=placed, out_specs=P("col", "row"), check_vma=False
    )
```

profile of v0, /device:TPU:2, one launch (start us, length us, event | category | flops | bytes accessed | tf_op | source)
XLA Modules:
  0.0 390.2 jit_solution(8472920669554600024)
XLA Ops:
  6.5 0.0 copy-start
  6.5 0.0 all-gather.3.cloned.1.call-start
  6.5 1.0 convert_reduce_fusion
  7.6 36.5 %psum.14 = f32[24]{0:T(128)S(1)} all-reduce(f32[24]{0:T(128)S(1)} %convert_reduce_fusion), channel_id=1, replica_groups=mesh['row'=16,'col'=32] {'row'}, use_global_device_ids=true, to_apply=%region_1.0 | all-reduce | flops 24 | bytes 192 | tf_op jit(solution)/shard_map/psum | solution.py:11
  44.1 1.0 fusion.10
  45.0 27.0 %psum.15 = f32[24]{0:T(128)S(1)} all-reduce(f32[24]{0:T(128)S(1)} %fusion.10), channel_id=1, replica_groups=mesh['row'=16,'col'=32] {'row'}, use_global_device_ids=true, to_apply=%region_3.0 | all-reduce | flops 24 | bytes 192 | tf_op jit(solution)/shard_map/psum | solution.py:14
  72.1 1.5 fusion.13
  73.6 0.0 all-gather.3.cloned.1.call-update
  73.6 0.0 reduce-scatter.3.cloned.1.call-start
  73.6 55.0 %all-gather.3.cloned.1.call-done = bf16[768,768]{1,0:T(8,128)(2,1)} async-done(((bf16[24,768]{1,0:T(8,128)(2,1)}), bf16[768,768]{1,0:T(8,128)(2,1)}) %all-gather.3.cloned.1.call-update) | async-done | bytes 1179664 | tf_op jit(solution)/shard_map/all_gather | solution.py:19
  128.7 0.0 copy-done
  128.7 4.7 %convolution_convert_fusion = bf16[768,1536]{1,0:T(8,128)(2,1)} fusion(bf16[768,768]{1,0:T(8,128)(2,1)} %all-gather.3.cloned.1.call-done, bf16[768,1536]{1,0:T(8,128)(2,1)S(1)} %copy-done), kind=kOutput, calls=%fused_computation | convolution fusion | flops 1813118976 | bytes 5898240 | tf_op jit(solution)/shard_map/dot_general | solution.py:21
  133.3 0.0 copy-start.2
  133.3 0.0 reduce-scatter.3.cloned.1.call-update
  133.4 0.0 all-gather.5.cloned.1.call-start
  133.4 73.7 %reduce-scatter.3.cloned.1.call-done = bf16[48,1536]{1,0:T(8,128)(2,1)} async-done(((bf16[768,1536]{1,0:T(8,128)(2,1)}), bf16[48,1536]{1,0:T(8,128)(2,1)}) %reduce-scatter.3.cloned.1.call-update) | async-done | bytes 147472 | tf_op jit(solution)/shard_map/reduce_scatter | solution.py:20
  207.1 0.0 copy-done.2
  207.1 1.7 fusion.7
  208.8 0.0 all-gather.5.cloned.1.call-update
  208.8 0.0 copy-start.1
  208.8 0.0 copy-start.3
  208.8 0.0 reduce-scatter.5.cloned.1.call-start
  208.9 72.3 %all-gather.5.cloned.1.call-done = bf16[768,1536]{1,0:T(8,128)(2,1)} async-done(((bf16[48,1536]{1,0:T(8,128)(2,1)}), bf16[768,1536]{1,0:T(8,128)(2,1)}) %all-gather.5.cloned.1.call-update) | async-done | bytes 2359312 | tf_op jit(solution)/shard_map/all_gather | solution.py:28
  281.1 5.4 %convolution_convert_fusion.1 = bf16[768,768]{1,0:T(8,128)(2,1)} fusion(bf16[768,1536]{1,0:T(8,128)(2,1)} %all-gather.5.cloned.1.call-done, bf16[1536,768]{1,0:T(8,128)(2,1)} %param.12), kind=kOutput, calls=%fused_computation.1 | convolution fusion | flops 1812529152 | bytes 5898240 | tf_op jit(solution)/shard_map/dot_general | solution.py:27
  286.5 0.0 reduce-scatter.5.cloned.1.call-update
  286.5 95.7 %reduce-scatter.5.cloned.1.call-done = bf16[24,768]{1,0:T(8,128)(2,1)} async-done(((bf16[768,768]{1,0:T(8,128)(2,1)}), bf16[24,768]{1,0:T(8,128)(2,1)}) %reduce-scatter.5.cloned.1.call-update) | async-done | bytes 36880 | tf_op jit(solution)/shard_map/reduce_scatter | solution.py:32
  382.3 0.0 copy-done.1
  382.3 0.0 copy-done.3
  382.3 1.4 fusion.15
  (2 shorter events, 0.0 us)
Async XLA Ops:
  6.5 122.1 %copy-start = (bf16[768,1536]{1,0:T(8,128)(2,1)S(1)}, bf16[768,1536]{1,0:T(8,128)(2,1)}, u32[]{:S(2)}) copy-start(bf16[768,1536]{1,0:T(8,128)(2,1)} %param.10) | copy-start | bytes 7077892
  6.5 122.1 %all-gather.3.cloned.1.call-start = ((), (), s32[]{:S(2)}) async-start(), calls=%async_computation.2 | async-start | bytes 1216512 | tf_op jit(solution)/shard_map/all_gather | solution.py:19
  73.6 133.5 %reduce-scatter.3.cloned.1.call-start = ((), (), s32[]{:S(2)}) async-start(), calls=%async_computation.3 | async-start | bytes 2506752 | tf_op jit(solution)/shard_map/reduce_scatter | solution.py:20
  133.3 73.8 %copy-start.2 = (f32[1536]{0:T(1024)S(1)}, f32[1536]{0:T(1024)}, u32[]{:S(2)}) copy-start(f32[1536]{0:T(1024)} %param.11) | copy-start | bytes 18436
  133.4 147.8 %all-gather.5.cloned.1.call-start = ((), (), s32[]{:S(2)}) async-start(), calls=%async_computation.4 | async-start | bytes 2506752 | tf_op jit(solution)/shard_map/all_gather | solution.py:28
  208.8 173.5 %copy-start.1 = (bf16[24,768]{1,0:T(8,128)(2,1)S(1)}, bf16[24,768]{1,0:T(8,128)(2,1)}, u32[]{:S(2)}) copy-start(bf16[24,768]{1,0:T(8,128)(2,1)} %param.7) | copy-start | bytes 110596
  208.8 173.5 %copy-start.3 = (f32[768]{0:T(1024)S(1)}, f32[768]{0:T(1024)}, u32[]{:S(2)}) copy-start(f32[768]{0:T(1024)} %param.13) | copy-start | bytes 9220
  208.8 173.4 %reduce-scatter.5.cloned.1.call-start = ((), (), s32[]{:S(2)}) async-start(), calls=%async_computation.5 | async-start | bytes 1216512 | tf_op jit(solution)/shard_map/reduce_scatter | solution.py:32
Sparse Core Ops, SparseCore 0:
  73.7 54.8 all-gather.2
  133.5 73.5 reduce-scatter.2
  209.2 71.9 all-gather.4
  286.7 95.5 reduce-scatter.4
where the time goes:
time: 391 us; the launch traced here: 390 us
  waiting for transfers between devices  297 us (76%)
  blocking collectives  63.5 us (16%)
  between operations  13.1 us (3%)
  matrix products  10.1 us (3%)
  other arithmetic  6.57 us (2%)
    reduce_scatter x1, waiting for transfers between devices, local(): lax.psum_scatter(terms.astype(jnp.bfloat16), 'col', scatter_dimension=0,...  95.7 us
    reduce_scatter x1, waiting for transfers between devices, local(): lax.psum_scatter(jnp.dot(gathered, w_up, preferred_element_type=jnp.float...  73.7 us
    all_gather x1, waiting for transfers between devices, local(): lax.all_gather(hidden, 'row', axis=0, tiled=True)  72.3 us
    all_gather x1, waiting for transfers between devices, local(): gathered = lax.all_gather(normed, 'col', axis=0, tiled=True)  55 us
    psum x1, blocking collectives, local(): total = lax.psum(jnp.sum(in_float, axis=1), 'row')  36.5 us
    psum x1, blocking collectives, local(): spread = lax.psum(jnp.sum(centered * centered, axis=1), 'row')  27 us
  transfers between devices with their start and end apart: 4, of which 4 were waited for; matrix products, arithmetic and copies ran while one was open for 0% of the time, Pallas kernels for 0%

commit v1 on v0

--- a/solution.py
+++ b/solution.py
@@ -2,6 +2,7 @@
 import jax.numpy as jnp
 from jax import lax
 from jax.sharding import PartitionSpec as P
+from jax.lax import all_to_all, axis_size
 
 D = 12288
 
@@ -16,7 +17,9 @@
     normed = (centered * lax.rsqrt(variance + 1e-05)[:, None] * ln_gain + ln_bias).astype(
         jnp.bfloat16
     )
-    gathered = lax.all_gather(normed, "col", axis=0, tiled=True)
+    gathered = jnp.concatenate(
+        all_to_all(jnp.stack(axis_size("col") * [normed], 0), "col", 0, 0), 0
+    )
     summed = lax.psum_scatter(
         jnp.dot(gathered, w_up, preferred_element_type=jnp.float32).astype(jnp.bfloat16),
         "row",

time: 391 us -> 354 us (0.905)
  waiting for transfers between devices: 297 us -> 236 us
  blocking collectives: 63.5 us -> 88.8 us
    all_gather x1 -> x0, waiting for transfers between devices: 55 us -> none  [local(): gathered = lax.all_gather(normed, 'col', axis=0, tiled=True)]
    all_to_all x0 -> x1, blocking collectives: none -> 25.3 us  [local(): all_to_all(jnp.stack(axis_size('col') * [normed], 0), 'col', 0, 0)]
    reduce_scatter x1, waiting for transfers between devices: 73.7 us -> 68 us  [local(): lax.psum_scatter(jnp.dot(gathered, w_up, preferred_element_type=jnp.float...]
  transfers between devices with their start and end apart: 4 -> 3, of which waited for: 4 -> 3; matrix products, arithmetic and copies ran while one was open for 0% -> 0% of each run, Pallas kernels for 0% -> 0%
where the time goes in v1:
time: 354 us; the launch traced here: 353 us
  waiting for transfers between devices  236 us (67%)
  blocking collectives  88.8 us (25%)
  between operations  13.1 us (4%)
  matrix products  8.78 us (2%)
  other arithmetic  5.96 us (2%)
    reduce_scatter x1, waiting for transfers between devices, local(): lax.psum_scatter(terms.astype(jnp.bfloat16), 'col', scatter_dimension=0,...  95.8 us
    all_gather x1, waiting for transfers between devices, local(): lax.all_gather(hidden, 'row', axis=0, tiled=True)  72.4 us
    reduce_scatter x1, waiting for transfers between devices, local(): lax.psum_scatter(jnp.dot(gathered, w_up, preferred_element_type=jnp.float...  68 us
    psum x1, blocking collectives, local(): total = lax.psum(jnp.sum(in_float, axis=1), 'row')  36.5 us
    psum x1, blocking collectives, local(): spread = lax.psum(jnp.sum(centered * centered, axis=1), 'row')  27 us
    all_to_all x1, blocking collectives, local(): all_to_all(jnp.stack(axis_size('col') * [normed], 0), 'col', 0, 0)  25.3 us
  transfers between devices with their start and end apart: 3, of which 3 were waited for; matrix products, arithmetic and copies ran while one was open for 0% of the time, Pallas kernels for 0%

profile of v1, /device:TPU:2, one launch (start us, length us, event | category | flops | bytes accessed | tf_op | source)
XLA Modules:
  0.0 353.1 jit_solution(11932974096498430015)
XLA Ops:
  6.5 0.0 copy-start
  6.5 0.0 reduce-scatter.3.cloned.1.call-start
  6.5 1.0 convert_reduce_fusion
  7.6 36.5 %psum.14 = f32[24]{0:T(128)S(1)} all-reduce(f32[24]{0:T(128)S(1)} %convert_reduce_fusion), channel_id=1, replica_groups=mesh['row'=16,'col'=32] {'row'}, use_global_device_ids=true, to_apply=%region_1.0 | all-reduce | flops 24 | bytes 192 | tf_op jit(solution)/shard_map/psum | solution.py:12
  44.1 1.0 fusion.10
  45.0 27.0 %psum.15 = f32[24]{0:T(128)S(1)} all-reduce(f32[24]{0:T(128)S(1)} %fusion.10), channel_id=1, replica_groups=mesh['row'=16,'col'=32] {'row'}, use_global_device_ids=true, to_apply=%region_3.0 | all-reduce | flops 24 | bytes 192 | tf_op jit(solution)/shard_map/psum | solution.py:15
  72.1 0.9 fusion.13
  73.0 0.1 stack.2
  73.0 25.3 %all_to_all.5 = bf16[32,24,768]{2,1,0:T(8,128)(2,1)S(1)} all-to-all(bf16[32,24,768]{2,1,0:T(8,128)(2,1)S(1)} %stack.2), channel_id=1, replica_groups=mesh['row'=16,'col'=32] {'col'}, dimensions={0} | all-to-all | bytes 2359296 | tf_op jit(solution)/shard_map/all_to_all | solution.py:21
  98.3 0.0 copy-done
  98.3 3.4 convolution_convert_fusion
  101.7 0.0 copy-start.2
  101.7 0.0 reduce-scatter.3.cloned.1.call-update
  101.7 0.0 all-gather.2.cloned.1.call-start
  101.8 68.0 %reduce-scatter.3.cloned.1.call-done = bf16[48,1536]{1,0:T(8,128)(2,1)} async-done(((bf16[768,1536]{1,0:T(8,128)(2,1)}), bf16[48,1536]{1,0:T(8,128)(2,1)}) %reduce-scatter.3.cloned.1.call-update) | async-done | bytes 147472 | tf_op jit(solution)/shard_map/reduce_scatter | solution.py:23
  169.8 0.0 copy-done.2
  169.8 1.7 fusion.7
  171.5 0.0 all-gather.2.cloned.1.call-update
  171.5 0.0 copy-start.1
  171.5 0.0 copy-start.3
  171.6 0.0 reduce-scatter.5.cloned.1.call-start
  171.6 72.4 %all-gather.2.cloned.1.call-done = bf16[768,1536]{1,0:T(8,128)(2,1)} async-done(((bf16[48,1536]{1,0:T(8,128)(2,1)}), bf16[768,1536]{1,0:T(8,128)(2,1)}) %all-gather.2.cloned.1.call-update) | async-done | bytes 2359312 | tf_op jit(solution)/shard_map/all_gather | solution.py:31
  244.0 5.4 %convolution_convert_fusion.1 = bf16[768,768]{1,0:T(8,128)(2,1)} fusion(bf16[768,1536]{1,0:T(8,128)(2,1)} %all-gather.2.cloned.1.call-done, bf16[1536,768]{1,0:T(8,128)(2,1)} %param.12), kind=kOutput, calls=%fused_computation.1 | convolution fusion | flops 1812529152 | bytes 5898240 | tf_op jit(solution)/shard_map/dot_general | solution.py:30
  249.4 0.0 reduce-scatter.5.cloned.1.call-update
  249.4 95.8 %reduce-scatter.5.cloned.1.call-done = bf16[24,768]{1,0:T(8,128)(2,1)} async-done(((bf16[768,768]{1,0:T(8,128)(2,1)}), bf16[24,768]{1,0:T(8,128)(2,1)}) %reduce-scatter.5.cloned.1.call-update) | async-done | bytes 36880 | tf_op jit(solution)/shard_map/reduce_scatter | solution.py:35
  345.2 0.0 copy-done.1
  345.2 0.0 copy-done.3
  345.2 1.4 fusion.15
  (2 shorter events, 0.0 us)
Async XLA Ops:
  6.5 91.8 %copy-start = (bf16[768,1536]{1,0:T(8,128)(2,1)S(1)}, bf16[768,1536]{1,0:T(8,128)(2,1)}, u32[]{:S(2)}) copy-start(bf16[768,1536]{1,0:T(8,128)(2,1)} %param.10) | copy-start | bytes 7077892
  6.5 163.3 %reduce-scatter.3.cloned.1.call-start = ((), (), s32[]{:S(2)}) async-start(), calls=%async_computation.3 | async-start | bytes 2506752 | tf_op jit(solution)/shard_map/reduce_scatter | solution.py:23
  101.7 68.1 %copy-start.2 = (f32[1536]{0:T(1024)S(1)}, f32[1536]{0:T(1024)}, u32[]{:S(2)}) copy-start(f32[1536]{0:T(1024)} %param.11) | copy-start | bytes 18436
  101.7 142.3 %all-gather.2.cloned.1.call-start = ((), (), s32[]{:S(2)}) async-start(), calls=%async_computation.4 | async-start | bytes 2506752 | tf_op jit(solution)/shard_map/all_gather | solution.py:31
  171.5 173.6 %copy-start.1 = (bf16[24,768]{1,0:T(8,128)(2,1)S(1)}, bf16[24,768]{1,0:T(8,128)(2,1)}, u32[]{:S(2)}) copy-start(bf16[24,768]{1,0:T(8,128)(2,1)} %param.7) | copy-start | bytes 110596
  171.5 173.6 %copy-start.3 = (f32[768]{0:T(1024)S(1)}, f32[768]{0:T(1024)}, u32[]{:S(2)}) copy-start(f32[768]{0:T(1024)} %param.13) | copy-start | bytes 9220
  171.6 173.6 %reduce-scatter.5.cloned.1.call-start = ((), (), s32[]{:S(2)}) async-start(), calls=%async_computation.5 | async-start | bytes 1216512 | tf_op jit(solution)/shard_map/reduce_scatter | solution.py:35
Sparse Core Ops, SparseCore 0:
  101.9 67.9 reduce-scatter.2
  171.9 72.0 all-gather.1
  249.5 95.5 reduce-scatter.4
